TPU v7x, 32 devices: a whole 2x2x4 slice. The times are simulated.
32 devices in a mesh: ctx: 8 (over z, x), dp: 4 (over y, core).
Axes of the slice: x: 2, y: 2, z: 4, core: 2. Of those that a mesh axis runs over, the one named last changes fastest.
Arguments:
- query: bfloat16 [4, 2048, 1024], P('dp', 'ctx'), may hold values from -6 to 6
- keys: bfloat16 [4, 2048, 128], P('dp', 'ctx'), may hold values from -6 to 6
- values: bfloat16 [4, 2048, 128], P('dp', 'ctx'), may hold values from -6 to 6
- attn_out: bfloat16 [4, 2048, 1024], P('dp', 'ctx'), may hold values from -6 to 6
- out_grad: bfloat16 [4, 2048, 1024], P('dp', 'ctx'), may hold values from -6 to 6
- lse: float32 [4, 8, 2048], P('dp', None, 'ctx'), may hold values from 4 to 7
- doc_start: int32 [4, 2048], P('dp', 'ctx'), may hold values from 0 to 2047, as said below
- inputs: bfloat16 [4, 2048, 4096], P('dp', 'ctx'), may hold values from -6 to 6
Outputs:
- query_grad: bfloat16 [4, 2048, 1024], P('dp', 'ctx')
- key_grad: bfloat16 [4, 2048, 128], P('dp', 'ctx')
- value_grad: bfloat16 [4, 2048, 128], P('dp', 'ctx')
- key_weight_grad: float32 [4096, 128], P('dp')
Inputs may be any that keep to these rules, and one draw needn't show every extreme that they name: doc_start[p, t] is the first position of the document that holds token t of pack p: it never falls along t, doc_start[p, t] <= t, it equals t exactly where a document begins, doc_start[p, 0] = 0, and the last position of every pack begins a document of its own; each pack holds the larger of 4 and 1 documents.
All inputs are finite; a program needn't handle non-finite values.
Results may differ from a plain program's by a relative error of at most 0.0055.
Values may be sent and summed in bfloat16 or wider, within the bound.
A program may use at most 64 MiB of HBM per device.

v0:
```python
import jax
import jax.numpy as jnp
from jax import lax
from jax.sharding import PartitionSpec as P

QH = 8
WINDOW = 256


def shifted(block, axis, distance):
    devices = range(lax.axis_size(axis))
    route = [(i - distance, i) for i in devices if i - distance in devices]
    return lax.ppermute(block, axis, route)


def grad_block(query, dout, lse, delta, qpos, qstart, keys, values, kpos):
    rows = query.shape[0]
    head_size = keys.shape[1]
    q_three = query.reshape(rows, QH, head_size)
    d_three = dout.reshape(rows, QH, head_size)
    scale = head_size ** (-0.5)
    scores = jnp.einsum("rhd,kd->hrk", q_three, keys, preferred_element_type=jnp.float32)
    allowed = (
        (kpos[None, :] >= qstart[:, None])
        & (kpos[None, :] <= qpos[:, None])
        & (qpos[:, None] - kpos[None, :] < WINDOW)
    )
    probs = jnp.where(allowed[None], jnp.exp(scores * scale - lse[:, :, None]), 0.0)
    probs_low = probs.astype(jnp.bfloat16)
    value_part = jnp.einsum("hrk,rhd->kd", probs_low, d_three, preferred_element_type=jnp.float32)
    dprob = jnp.einsum("rhd,kd->hrk", d_three, values, preferred_element_type=jnp.float32)
    score_grad = (probs * (dprob - delta[:, :, None]) * scale).astype(jnp.bfloat16)
    query_part = jnp.einsum(
        "hrk,kd->rhd", score_grad, keys, preferred_element_type=jnp.float32
    ).reshape(rows, QH * head_size)
    key_part = jnp.einsum("hrk,rhd->kd", score_grad, q_three, preferred_element_type=jnp.float32)
    return (query_part, key_part, value_part)


def local(query, keys, values, attn_out, out_grad, lse, doc_start, inputs):
    q_rows = query[0]
    k_rows = keys[0]
    v_rows = values[0]
    d_rows = out_grad[0]
    lse_rows = lse[0]
    starts = doc_start[0]
    layer_in = inputs[0]
    rows = q_rows.shape[0]
    head_size = k_rows.shape[1]
    shard = lax.axis_index("ctx")
    places = shard * rows + jnp.arange(rows, dtype=jnp.int32)
    delta = jnp.sum(
        (d_rows.astype(jnp.float32) * attn_out[0].astype(jnp.float32)).reshape(rows, QH, head_size),
        axis=-1,
    ).T
    dq, dk, dv = grad_block(q_rows, d_rows, lse_rows, delta, places, starts, k_rows, v_rows, places)
    tail = rows - WINDOW
    prev_keys, prev_values = shifted((k_rows, v_rows), "ctx", 1)
    prev_places = shard * rows - WINDOW + jnp.arange(WINDOW, dtype=jnp.int32)
    near_q, near_k, near_v = grad_block(
        q_rows, d_rows, lse_rows, delta, places, starts, prev_keys, prev_values, prev_places
    )
    dq = dq.at[:WINDOW].add(near_q)
    back_keys, back_values = shifted((near_k, near_v), "ctx", -1)
    dk = dk.at[tail:].add(back_keys)
    dv = dv.at[tail:].add(back_values)
    dk_low = dk.astype(jnp.bfloat16)
    pack_sum = lax.psum_scatter(
        lax.dot_general(
            layer_in, dk_low, (((0,), (0,)), ((), ())), preferred_element_type=jnp.float32
        ),
        "dp",
        scatter_dimension=0,
        tiled=True,
    )
    total = lax.psum(pack_sum, "ctx")
    return (dq.astype(jnp.bfloat16)[None], dk_low[None], dv.astype(jnp.bfloat16)[None], total)


def solution(mesh):
    in_specs = (
        P("dp", "ctx", None),
        P("dp", "ctx", None),
        P("dp", "ctx", None),
        P("dp", "ctx", None),
        P("dp", "ctx", None),
        P("dp", None, "ctx"),
        P("dp", "ctx"),
        P("dp", "ctx", None),
    )
    out_specs = (P("dp", "ctx", None), P("dp", "ctx", None), P("dp", "ctx", None), P("dp", None))
    return jax.shard_map(local, mesh=mesh, in_specs=in_specs, out_specs=out_specs, check_vma=False)
```

profile of v0, /device:TPU:0, one launch (start us, length us, event | category | flops | bytes accessed | tf_op | source)
XLA Modules:
  0.0 150.4 jit_solution(18366470658442900688)
XLA Ops:
  7.2 5.0 %collective-permute-start = (bf16[256,128]{1,0:T(8,128)(2,1)}, bf16[256,128]{1,0:T(8,128)(2,1)S(1)}, u32[]{:S(2)}, u32[]{:S(2)}) collective-permute-start(bf16[256,128]{1,0:T(8,128)(2,1)} %bitcast.112), channel_id=1, source_target_pairs={{0,4},{4,8},{8,12},{12,16},{16,20},{20,24},{24,28},{1,5},{5,9},{9,... | collective-permute-start | bytes 196616 | tf_op jit(solution)/shard_map/ppermute | solution.py:13
  12.2 3.5 %collective-permute-start.1 = (bf16[256,128]{1,0:T(8,128)(2,1)}, bf16[256,128]{1,0:T(8,128)(2,1)S(1)}, u32[]{:S(2)}, u32[]{:S(2)}) collective-permute-start(bf16[256,128]{1,0:T(8,128)(2,1)} %bitcast.111), channel_id=1, source_target_pairs={{0,4},{4,8},{8,12},{12,16},{16,20},{20,24},{24,28},{1,5},{5,9},{9,... | collective-permute-start | bytes 196616 | tf_op jit(solution)/shard_map/ppermute | solution.py:13
  15.7 1.2 copy.47
  16.9 1.1 copy.48
  19.0 1.9 %fusion.10 = f32[8,256,256]{1,2,0:T(8,128)} fusion(f32[8,256]{1,0:T(8,128)S(1)} %bitcast.114, pred[256,256]{0,1:T(8,128)(4,1)S(1)} %get-tuple-element.73, bf16[256,8,128]{2,1,0:T(8,128)(2,1)S(1)} %bitcast.102, bf16[1,256,128]{2,1,0:T(8,128)(2,1)S(1)} %copy-done.10), kind=kOutput, calls=%fused_computation.15 | convolution fusion | flops 135790592 | bytes 2760704 | tf_op jit(solution)/shard_map/rhd,kd->hrk/dot_general | solution.py:22
  21.3 0.6 fusion.5
  22.0 0.5 fusion.3
  22.5 0.4 convolution_bitcast_fusion.3
  22.9 0.4 copy-done.3
  23.3 1.4 collective-permute-start.2
  24.8 0.5 fusion.8
  25.2 5.1 %collective-permute-done.2 = f32[256,128]{1,0:T(8,128)S(1)} collective-permute-done((f32[256,128]{1,0:T(8,128)S(1)}, f32[256,128]{1,0:T(8,128)S(1)}, u32[]{:S(2)}, u32[]{:S(2)}) %collective-permute-start.2) | collective-permute-done | bytes 131104 | tf_op jit(solution)/shard_map/ppermute | solution.py:13
  30.3 0.4 fusion.15
  30.7 1.8 %convolution_bitcast_fusion = f32[4096,128]{0,1:T(8,128)} fusion(bf16[256,128]{1,0:T(8,128)(2,1)S(1)} %fusion.15, bf16[1,256,4096]{2,1,0:T(8,128)(2,1)S(1)} %copy-done), kind=kOutput, calls=%fused_computation | convolution fusion | flops 268435456 | bytes 4259840 | tf_op jit(solution)/shard_map/dot_general | solution.py:69
  32.6 2.6 %fusion.33 = f32[8,256,128]{1,2,0:T(8,128)} fusion(bf16[8,256,256]{1,2,0:T(8,128)(2,1)} %copy-done.1, bf16[1,256,128]{2,1,0:T(8,128)(2,1)S(1)} %copy-done.10), kind=kOutput, calls=%fused_computation.47 | convolution fusion | flops 134217728 | bytes 2162688 | tf_op jit(solution)/shard_map/hrk,kd->rhd/dot_general | solution.py:33
  35.3 30.1 %reduce-scatter.2.cloned.1.call-done = f32[1024,128]{0,1:T(8,128)} async-done(((f32[4096,128]{0,1:T(8,128)}), f32[1024,128]{0,1:T(8,128)}) %reduce-scatter.2.cloned.1.call-update) | async-done | bytes 524304 | tf_op jit(solution)/shard_map/reduce_scatter | solution.py:68
  65.4 2.2 %convolution_bitcast_fusion.1 = f32[256,128]{1,0:T(8,128)S(1)} fusion(f32[8,256,256]{1,2,0:T(8,128)} %copy-done.3, bf16[256,8,128]{2,1,0:T(8,128)(2,1)S(1)} %bitcast.99), kind=kOutput, calls=%fused_computation.18 | convolution fusion | flops 134742016 | bytes 2752512 | tf_op jit(solution)/shard_map/hrk,rhd->kd/dot_general | solution.py:30
  67.5 1.3 collective-permute-start.3
  68.9 0.4 fusion.11
  69.2 1.0 copy.39
  70.2 4.4 %collective-permute-done.3 = f32[256,128]{1,0:T(8,128)S(1)} collective-permute-done((f32[256,128]{1,0:T(8,128)S(1)}, f32[256,128]{1,0:T(8,128)S(1)}, u32[]{:S(2)}, u32[]{:S(2)}) %collective-permute-start.3) | collective-permute-done | bytes 131104 | tf_op jit(solution)/shard_map/ppermute | solution.py:13
  74.7 2.7 %fusion.16 = bf16[1,256,128]{2,1,0:T(8,128)(2,1)} fusion(f32[256,128]{1,0:T(8,128)S(1)} %collective-permute-done.3, f32[8,256,256]{1,2,0:T(8,128)} %fusion.10, bf16[256,8,128]{2,1,0:T(8,128)(2,1)S(1)} %bitcast.100), kind=kOutput, calls=%fused_computation.26 | convolution fusion | flops 134807552 | bytes 2818048 | tf_op jit(solution)/shard_map/hrk,rhd->kd/dot_general | solution.py:30
  77.3 64.2 %all-reduce.2.cloned.1.call-done = f32[1024,128]{0,1:T(8,128)} async-done(((f32[1024,128]{0,1:T(8,128)}), f32[1024,128]{0,1:T(8,128)}) %all-reduce.2.cloned.1.call-update) | async-done | bytes 524304 | tf_op jit(solution)/shard_map/psum | solution.py:76
  141.5 2.0 %copy.40 = f32[1024,128]{1,0:T(8,128)} copy(f32[1024,128]{0,1:T(8,128)} %all-reduce.2.cloned.1.call-done) | data formatting | bytes 1048576
  (37 shorter events, 1.4 us)
Async XLA Ops:
  7.2 23.6 %copy-start = (bf16[1,256,4096]{2,1,0:T(8,128)(2,1)S(1)}, bf16[1,256,4096]{2,1,0:T(8,128)(2,1)}, u32[]{:S(2)}) copy-start(bf16[1,256,4096]{2,1,0:T(8,128)(2,1)} %param.27) | copy-start | bytes 6291460
  7.2 58.1 %reduce-scatter.2.cloned.1.call-start = ((), (), s32[]{:S(2)}) async-start(), calls=%async_computation.1 | async-start | bytes 2621440 | tf_op jit(solution)/shard_map/reduce_scatter | solution.py:68
  7.2 14.1 %collective-permute-start = (bf16[256,128]{1,0:T(8,128)(2,1)}, bf16[256,128]{1,0:T(8,128)(2,1)S(1)}, u32[]{:S(2)}, u32[]{:S(2)}) collective-permute-start(bf16[256,128]{1,0:T(8,128)(2,1)} %bitcast.112), channel_id=1, source_target_pairs={{0,4},{4,8},{8,12},{12,16},{16,20},{20,24},{24,28},{1,5},{5,9},{9,... | collective-permute-start | bytes 196616 | tf_op jit(solution)/shard_map/ppermute | solution.py:13
  12.2 9.8 %collective-permute-start.1 = (bf16[256,128]{1,0:T(8,128)(2,1)}, bf16[256,128]{1,0:T(8,128)(2,1)S(1)}, u32[]{:S(2)}, u32[]{:S(2)}) collective-permute-start(bf16[256,128]{1,0:T(8,128)(2,1)} %bitcast.111), channel_id=1, source_target_pairs={{0,4},{4,8},{8,12},{12,16},{16,20},{20,24},{24,28},{1,5},{5,9},{9,... | collective-permute-start | bytes 196616 | tf_op jit(solution)/shard_map/ppermute | solution.py:13
  15.7 2.4 %copy-start.7 = (bf16[1,256,1024]{2,1,0:T(8,128)(2,1)S(1)}, bf16[1,256,1024]{2,1,0:T(8,128)(2,1)}, u32[]{:S(2)}) copy-start(bf16[1,256,1024]{2,1,0:T(8,128)(2,1)} %param.23) | copy-start | bytes 1572868
  18.1 0.7 copy-start.11
  18.1 0.9 copy-start.10
  18.1 0.9 copy-start.12
  22.0 1.3 copy-start.3
  22.0 2.7 %copy-start.2 = (f32[8,256,256]{1,2,0:T(8,128)S(1)}, f32[8,256,256]{1,2,0:T(8,128)}, u32[]{:S(2)}) copy-start(f32[8,256,256]{1,2,0:T(8,128)} %fusion.10) | copy-start | bytes 6291460
  22.0 2.7 %copy-start.9 = (bf16[1,256,128]{2,1,0:T(8,128)(2,1)S(1)}, bf16[1,256,128]{2,1,0:T(8,128)(2,1)}, u32[]{:S(2)}) copy-start(bf16[1,256,128]{2,1,0:T(8,128)(2,1)} %param.22) | copy-start | bytes 196612
  22.5 2.7 %copy-start.4 = (bf16[8,256,256]{1,2,0:T(8,128)(2,1)}, bf16[8,256,256]{1,2,0:T(8,128)(2,1)S(1)}, u32[]{:S(2)}) copy-start(bf16[8,256,256]{1,2,0:T(8,128)(2,1)S(1)} %fusion.3) | copy-start | bytes 3145732
  23.3 7.0 %collective-permute-start.2 = (f32[256,128]{1,0:T(8,128)S(1)}, f32[256,128]{1,0:T(8,128)S(1)}, u32[]{:S(2)}, u32[]{:S(2)}) collective-permute-start(f32[256,128]{1,0:T(8,128)S(1)} %convolution_bitcast_fusion.3), channel_id=1, source_target_pairs={{4,0},{8,4},{12,8},{16,12},{20,16},{24,20},{28,24},{5,1},{9,5},{13... | collective-permute-start | bytes 393224 | tf_op jit(solution)/shard_map/ppermute | solution.py:13
  25.2 5.1 %copy-start.1 = (bf16[8,256,256]{1,2,0:T(8,128)(2,1)}, bf16[8,256,256]{1,2,0:T(8,128)(2,1)S(1)}, u32[]{:S(2)}) copy-start(bf16[8,256,256]{1,2,0:T(8,128)(2,1)S(1)} %fusion.8) | copy-start | bytes 3145732
  30.7 1.8 %copy-start.8 = (bf16[256,128]{1,0:T(8,128)(2,1)}, bf16[256,128]{1,0:T(8,128)(2,1)S(1)}, u32[]{:S(2)}) copy-start(bf16[256,128]{1,0:T(8,128)(2,1)S(1)} %fusion.15) | copy-start | bytes 196612
  32.6 108.9 %all-reduce.2.cloned.1.call-start = ((), (), s32[]{:S(2)}) async-start(), calls=%async_computation.2 | async-start | bytes 1048576 | tf_op jit(solution)/shard_map/psum | solution.py:76
  65.3 3.5 %copy-start.5 = (bf16[8,256,256]{1,2,0:T(8,128)(2,1)S(1)}, bf16[8,256,256]{1,2,0:T(8,128)(2,1)}, u32[]{:S(2)}) copy-start(bf16[8,256,256]{1,2,0:T(8,128)(2,1)} %copy-done.4) | copy-start | bytes 3145732
  65.4 3.5 %copy-start.6 = (f32[8,256,128]{1,2,0:T(8,128)S(1)}, f32[8,256,128]{1,2,0:T(8,128)}, u32[]{:S(2)}) copy-start(f32[8,256,128]{1,2,0:T(8,128)} %fusion.33) | copy-start | bytes 3145732
  67.5 7.1 %collective-permute-start.3 = (f32[256,128]{1,0:T(8,128)S(1)}, f32[256,128]{1,0:T(8,128)S(1)}, u32[]{:S(2)}, u32[]{:S(2)}) collective-permute-start(f32[256,128]{1,0:T(8,128)S(1)} %convolution_bitcast_fusion.1), channel_id=1, source_target_pairs={{4,0},{8,4},{12,8},{16,12},{20,16},{24,20},{28,24},{5,1},{9,5},{13... | collective-permute-start | bytes 393224 | tf_op jit(solution)/shard_map/ppermute | solution.py:13
Sparse Core Ops, SparseCore 0:
  32.7 32.5 reduce-scatter.1
  69.1 72.3 all-reduce.1
where the time goes:
time: 151 us; the launch traced here: 150 us
  waiting for transfers between devices  104 us (69%)
  between operations  14.4 us (10%)
  matrix products  14 us (9%)
  starting transfers between devices  11.2 us (7%)
  local copies, waits for them, and re-layouts  6.4 us (4%)
    psum x1, waiting for transfers between devices, local(): total = lax.psum(pack_sum, 'ctx')  64.2 us
    reduce_scatter x1, waiting for transfers between devices, local(): lax.psum_scatter(lax.dot_general(layer_in, dk_low, (((0,), (0,)), ((), ()...  30.1 us
    ppermute x4, starting transfers between devices, shifted(): return lax.ppermute(block, axis, route)  11.1 us
    ppermute x4, waiting for transfers between devices, shifted(): return lax.ppermute(block, axis, route)  9.51 us
    unnamed x31, local copies, waits for them, and re-layouts  6.34 us
    dot_general x2, matrix products, grad_block(): jnp.einsum('hrk,rhd->kd', probs_low, d_three, preferred_element_type=jnp....  4.83 us
  transfers between devices with their start and end apart: 6, of which 4 were waited for; matrix products, arithmetic and copies ran while one was open for 10% of the time, Pallas kernels for 0%

commit v1 on v0

v1 whole, which is shorter than its diff:
```python
import functools

import jax
import jax.numpy as jnp
from jax import lax
from jax.experimental import pallas as pl
from jax.experimental.pallas import tpu as pltpu
from jax.sharding import PartitionSpec as P

QH = 8
WINDOW = 256
F32 = jnp.float32
BF16 = jnp.bfloat16
NT = (((1,), (1,)), ((), ()))


def dot(a, b):
    return jnp.dot(a, b, preferred_element_type=F32)


def dot_nt(a, b):
    return lax.dot_general(a, b, NT, preferred_element_type=F32)


def remote(src, dst, send, recv, where):
    return pltpu.make_async_remote_copy(
        src_ref=src, dst_ref=dst, send_sem=send, recv_sem=recv,
        device_id=where, device_id_type=pl.DeviceIdType.MESH,
    )


def kernel(n_ctx, n_dp, reduce_here, *refs):
    (q_in, k_in, v_in, o_in, g_in, lse_in, start_in, x_in) = refs[:8]
    n_out = 4 if reduce_here else 3
    outs = refs[8:8 + n_out]
    dq_out, dk_out, dv_out = outs[:3]
    scratch = refs[8 + n_out:]
    (q, k, v, o, g, lse, start, delta, kp, vp, ds_all, dq, dk_own, dv_own, dk_near, dv_near,
     dk_send, dv_send, dk_back, dv_back, dk_low, dv_low, load, store, halo_s, halo_r, back_s, back_r) = scratch[:28]
    rows, width = q.shape
    head = width // QH
    scale = head ** (-0.5)
    c = lax.axis_index("ctx")
    d = lax.axis_index("dp")
    after = lax.rem(c + 1, n_ctx)
    before = lax.rem(c + n_ctx - 1, n_ctx)

    loads = [
        pltpu.make_async_copy(src.at[0], dst, load.at[i])
        for i, (src, dst) in enumerate(
            ((k_in, k), (v_in, v), (q_in, q), (g_in, g), (o_in, o), (lse_in, lse))
        )
    ]
    loads.append(pltpu.make_async_copy(start_in, start, load.at[6]))
    for copy in loads:
        copy.start()

    partners = [(after, d), (before, d)]
    if reduce_here:
        (tot_out,) = outs[3:]
        (xl, xr, dkt, dkt_r, wf, s1, r1, s2, r2, s3, r3, gb, tot,
         xload, x_s, x_r, t_s, t_r, p1_s, p1_r, p2_s, p2_r, p3_s, p3_r, ag_s, ag_r) = scratch[28:]
        nz = n_ctx // 2
        block = x_in.shape[2] // n_dp
        core, y = lax.rem(d, 2), d // 2
        xx, z = lax.rem(c, 2), c // 2
        at_core = (c, y * 2 + 1 - core)
        at_y = (c, (1 - y) * 2 + core)
        at_x = (z * 2 + 1 - xx, d)
        at_z = [(lax.rem(z + s + 1, nz) * 2 + xx, d) for s in range(nz - 1)]
        partners += [at_core, at_y, at_x] + at_z
    barrier = pltpu.get_barrier_semaphore()
    for where in partners:
        pl.semaphore_signal(barrier, inc=1, device_id=where, device_id_type=pl.DeviceIdType.MESH)
    pl.semaphore_wait(barrier, len(partners))

    halo = [
        remote(src.at[0], dst, halo_s.at[i], halo_r.at[i], (after, d))
        for i, (src, dst) in enumerate(((k_in, kp), (v_in, vp)))
    ]
    for copy in halo:
        copy.start()
    if reduce_here:
        xcopies = []
        for yy in range(2):
            mine = pl.ds(pl.multiple_of((yy * 2 + core) * block, block), block)
            other = pl.ds(pl.multiple_of((yy * 2 + 1 - core) * block, block), block)
            xcopies.append(pltpu.make_async_copy(x_in.at[0, :, mine], xl.at[yy], xload.at[yy]))
            xcopies.append(remote(x_in.at[0, :, other], xr.at[yy], x_s.at[yy], x_r.at[yy], at_core))
        for copy in xcopies:
            copy.start()

    for copy in loads:
        copy.wait()
    lane = lax.broadcasted_iota(jnp.int32, (rows, 128), 1)
    spread = jnp.zeros((rows, 128), F32)
    for h in range(QH):
        cols = slice(h * head, (h + 1) * head)
        one = jnp.sum(g[:, cols].astype(F32) * o[:, cols].astype(F32), axis=1, keepdims=True)
        spread = jnp.where(lane == h, one, spread)
    delta[...] = spread.T[:QH]

    s_at = lax.broadcasted_iota(jnp.int32, (rows, rows), 0)
    t_at = lax.broadcasted_iota(jnp.int32, (rows, rows), 1)
    first = start[...] - c * rows

    def part(keys, values, allowed, base, dk_sum, dv_sum):
        def one(h):
            cols = pl.ds(pl.multiple_of(h * head, head), head)
            qh, gh = q[:, cols], g[:, cols]
            s = dot_nt(keys[...], qh)
            dp = dot_nt(values[...], gh)
            p = jnp.where(allowed, jnp.exp(s * scale - lse[pl.ds(h, 1), :]), 0.0)
            low = p.astype(BF16)
            sg = (p * (dp - delta[pl.ds(h, 1), :]) * scale).astype(BF16)
            ds_all[h, base:base + rows, :] = sg
            return dot(sg, qh), dot(low, gh)

        def body(i, carry):
            a, b = one(2 * i), one(2 * i + 1)
            dk_sum[...] += a[0] + b[0]
            dv_sum[...] += a[1] + b[1]
            return carry

        dk_sum[...] = jnp.zeros_like(dk_sum)
        dv_sum[...] = jnp.zeros_like(dv_sum)
        lax.fori_loop(0, QH // 2, body, 0)

    part(k, v, (s_at >= first) & (s_at <= t_at), 0, dk_own, dv_own)
    for copy in halo:
        copy.wait()
    part(kp, vp, (s_at - WINDOW >= first) & (t_at - s_at + WINDOW < WINDOW), rows, dk_near, dv_near)
    dk_send[...] = dk_near[...].astype(BF16)
    back = [
        remote(src, dst, back_s.at[i], back_r.at[i], (before, d))
        for i, (src, dst) in enumerate(((dk_send, dk_back), (dv_send, dv_back)))
    ]
    back[0].start()
    dv_send[...] = dv_near[...].astype(BF16)
    back[1].start()

    kt = jnp.concatenate([k[...].astype(F32).T, kp[...].astype(F32).T], axis=1).astype(BF16)

    def dq_body(i, carry):
        for h in (2 * i, 2 * i + 1):
            cols = pl.ds(pl.multiple_of(h * head, head), head)
            dq[:, cols] = dot(kt, ds_all[h]).T.astype(BF16)
        return carry

    lax.fori_loop(0, QH // 2, dq_body, 0)
    dq_store = pltpu.make_async_copy(dq, dq_out.at[0], store.at[0])
    dq_store.start()

    back[0].wait()
    dk = dk_own[...] + dk_back[...].astype(F32)
    dk_low[...] = dk.astype(BF16)
    dk_store = pltpu.make_async_copy(dk_low, dk_out.at[0], store.at[1])

    if reduce_here:
        dkt[...] = dk.T.astype(BF16)
        trade = remote(dkt, dkt_r, t_s.at[0], t_r.at[0], at_core)
        trade.start()
    dk_store.start()

    def finish_dv():
        back[1].wait()
        dv_low[...] = (dv_own[...] + dv_back[...].astype(F32)).astype(BF16)
        copy = pltpu.make_async_copy(dv_low, dv_out.at[0], store.at[2])
        copy.start()
        return copy

    if reduce_here:
        half = nz // 2
        for copy in xcopies:
            copy.wait()

        def pieces(yy, lo, hi, src, left, first_time):
            got = dot(left[...], src[yy, :, lo * 128:hi * 128])
            for j in range(lo, hi):
                piece = got[:, (j - lo) * 128:(j - lo + 1) * 128]
                if first_time:
                    wf[yy, j] = piece
                else:
                    wf[yy, j] += piece

        for yy in range(2):
            pieces(yy, 0, n_ctx, xl, dkt, True)
        trade.wait()
        for yy in range(2):
            pieces(yy, 0, n_ctx, xr, dkt_r, False)

        for j in range(n_ctx // 2):
            s1[0, j] = wf[1 - y, j].astype(BF16)
        e1 = [remote(s1.at[0], r1.at[0], p1_s.at[0], p1_r.at[0], at_y)]
        e1[0].start()
        for yy in range(2):
            for j in range(half):
                s1[1, yy * half + j] = wf[yy, (half + j) * 2 + 1 - xx].astype(BF16)
        e1.append(remote(s1.at[1], r1.at[1], p1_s.at[1], p1_r.at[1], at_x))
        e1[1].start()
        dv_store = finish_dv()

        e1[0].wait()
        for j in range(half):
            at = 2 * j + 1 - xx
            s2[0, j] = (wf[y, at] + r1[0, at].astype(F32)).astype(BF16)
        e2 = [remote(s2.at[0], r2.at[0], p2_s.at[0], p2_r.at[0], at_x)]
        e2[0].start()
        e1[1].wait()
        for j in range(half):
            at = (half + j) * 2 + xx
            s2[1, j] = (wf[1 - y, at] + r1[1, (1 - y) * half + j].astype(F32)).astype(BF16)
        e2.append(remote(s2.at[1], r2.at[1], p2_s.at[1], p2_r.at[1], at_y))
        e2[1].start()
        e2[0].wait()
        for j in range(half):
            at = 2 * j + xx
            s3[j] = wf[y, at] + r1[0, at].astype(F32) + r2[0, j].astype(F32)
        e2[1].wait()
        for j in range(half):
            at = (half + j) * 2 + xx
            s3[half + j] = wf[y, at] + r1[1, y * half + j].astype(F32) + r2[1, j].astype(F32)

        e3 = []
        for s in range(nz - 1):
            there = lax.rem(z + s + 1, nz)
            s1[0, s] = s3[there].astype(BF16)
            e3.append(remote(s1.at[0, s], r3.at[nz - 2 - s], p3_s.at[s], p3_r.at[nz - 2 - s], at_z[s]))
            e3[s].start()
        total = s3[z]
        for s in range(nz - 1):
            e3[s].wait_send()
        for s in range(nz - 1):
            e3[nz - 2 - s].wait_recv()
            total = total + r3[s].astype(F32)
        gb[c] = total.T.astype(BF16)

        sends = []
        over_z = [
            remote(gb.at[c], gb.at[c], ag_s.at[s], ag_r.at[s], at_z[s]) for s in range(nz - 1)
        ]
        own_x = remote(gb.at[c], gb.at[c], ag_s.at[nz - 1], ag_r.at[nz - 1], at_x)
        for copy in over_z:
            copy.start()
        own_x.start()
        passed = []
        for s in range(nz - 1):
            over_z[s].wait_recv()
            slot = lax.rem(z - s - 1 + nz, nz) * 2 + xx
            copy = remote(gb.at[slot], gb.at[slot], ag_s.at[nz + s], ag_r.at[nz + s], at_x)
            copy.start()
            passed.append(copy)
        own_x.wait_recv()
        for copy in passed:
            copy.wait_recv()
        tot[...] = gb[...].astype(F32).reshape(tot.shape)
        tot_store = pltpu.make_async_copy(tot, tot_out, store.at[3])
        tot_store.start()
        for copy in over_z + [own_x] + passed:
            copy.wait_send()
        tot_store.wait()
    else:
        dv_store = finish_dv()
    dq_store.wait()
    dk_store.wait()
    dv_store.wait()


def local(n_ctx, n_dp, query, keys, values, attn_out, out_grad, lse, doc_start, inputs):
    _, rows, width = query.shape
    head = width // QH
    depth = inputs.shape[2]
    reduce_here = n_dp == 4 and n_ctx % 4 == 0 and depth == n_dp * n_ctx * 128 and head == 128
    nz = n_ctx // 2
    any_space = pl.BlockSpec(memory_space=pl.ANY)
    out_shape = [
        jax.ShapeDtypeStruct(query.shape, BF16),
        jax.ShapeDtypeStruct(keys.shape, BF16),
        jax.ShapeDtypeStruct(keys.shape, BF16),
    ]
    dma = pltpu.SemaphoreType.DMA
    small = pltpu.VMEM((rows, head), BF16)
    wide = pltpu.VMEM((rows, head), F32)
    full = pltpu.VMEM((rows, width), BF16)
    scratch = [
        full, small, small, full, full, pltpu.VMEM((QH, rows), F32), pltpu.VMEM((1, rows), jnp.int32),
        pltpu.VMEM((QH, rows), F32), small, small, pltpu.VMEM((QH, 2 * rows, rows), BF16), full,
        wide, wide, wide, wide, small, small, small, small, small, small,
        dma((7,)), dma((4,)), dma((2,)), dma((2,)), dma((2,)), dma((2,)),
    ]
    if reduce_here:
        out_shape.append(jax.ShapeDtypeStruct((depth // n_dp, head), F32))
        scratch += [
            pltpu.VMEM((2, rows, depth // n_dp), BF16), pltpu.VMEM((2, rows, depth // n_dp), BF16),
            pltpu.VMEM((head, rows), BF16), pltpu.VMEM((head, rows), BF16),
            pltpu.VMEM((2, n_ctx, 128, 128), F32),
            pltpu.VMEM((2, nz, 128, 128), BF16), pltpu.VMEM((2, nz, 128, 128), BF16),
            pltpu.VMEM((2, nz // 2, 128, 128), BF16), pltpu.VMEM((2, nz // 2, 128, 128), BF16),
            pltpu.VMEM((nz, 128, 128), F32), pltpu.VMEM((nz - 1, 128, 128), BF16),
            pltpu.VMEM((n_ctx, 128, 128), BF16), pltpu.VMEM((depth // n_dp, head), F32),
            dma((2,)), dma((2,)), dma((2,)), dma((1,)), dma((1,)), dma((2,)), dma((2,)), dma((2,)), dma((2,)),
            dma((nz - 1,)), dma((nz - 1,)), dma((n_ctx - 1,)), dma((n_ctx - 1,)),
        ]
    got = pl.pallas_call(
        functools.partial(kernel, n_ctx, n_dp, reduce_here),
        out_shape=out_shape,
        in_specs=[any_space] * 8,
        out_specs=[any_space] * len(out_shape),
        scratch_shapes=scratch,
        compiler_params=pltpu.CompilerParams(
            collective_id=0, has_side_effects=True, vmem_limit_bytes=32 * 1024 * 1024
        ),
    )(query, keys, values, attn_out, out_grad, lse, doc_start, inputs)
    if reduce_here:
        return tuple(got)
    dq, dk, dv = got
    term = lax.dot_general(
        inputs[0], dk[0], (((0,), (0,)), ((), ())), preferred_element_type=jnp.float32
    )
    return dq, dk, dv, lax.psum(lax.psum_scatter(term, "dp", scatter_dimension=0, tiled=True), "ctx")


def solution(mesh):
    in_specs = (
        P("dp", "ctx", None),
        P("dp", "ctx", None),
        P("dp", "ctx", None),
        P("dp", "ctx", None),
        P("dp", "ctx", None),
        P("dp", None, "ctx"),
        P("dp", "ctx"),
        P("dp", "ctx", None),
    )
    out_specs = (P("dp", "ctx", None), P("dp", "ctx", None), P("dp", "ctx", None), P("dp", None))
    return jax.shard_map(
        functools.partial(local, mesh.shape["ctx"], mesh.shape["dp"]),
        mesh=mesh, in_specs=in_specs, out_specs=out_specs, check_vma=False,
    )
```

time: 151 us -> 50.8 us (0.34)
  waiting for transfers between devices: 104 us -> 0 us
  Pallas kernels: 0 us -> 39.1 us
  matrix products: 14 us -> 0 us
  between operations: 14.4 us -> 0.66 us
  starting transfers between devices: 11.2 us -> 0 us
  local copies, waits for them, and re-layouts: 6.4 us -> 10.6 us
    psum x1 -> x0, waiting for transfers between devices: 64.2 us -> none  [local(): total = lax.psum(pack_sum, 'ctx')]
    pallas_call x0 -> x1, Pallas kernels: none -> 39.1 us  [local(): pl.pallas_call(functools.partial(kernel, n_ctx, n_dp, reduce_here), out_s...]
    reduce_scatter x1 -> x0, waiting for transfers between devices: 30.1 us -> none  [local(): lax.psum_scatter(lax.dot_general(layer_in, dk_low, (((0,), (0,)), ((), ()...]
    dot_general x11 -> x0, matrix products: 14 us -> none  [the longest x2 4.83 us: grad_block(): jnp.einsum('hrk,rhd->kd', probs_low, d_three, preferred_element_type=jnp....]
    ppermute x4 -> x0, starting transfers between devices: 11.1 us -> none  [shifted(): return lax.ppermute(block, axis, route)]
    ppermute x4 -> x0, waiting for transfers between devices: 9.51 us -> none  [shifted(): return lax.ppermute(block, axis, route)]
    unnamed x31 -> x20, local copies, waits for them, and re-layouts: 6.34 us -> 10.6 us
  transfers between devices with their start and end apart: 6 -> 0, of which waited for: 4 -> 0; matrix products, arithmetic and copies ran while one was open for 10% -> 0% of each run, Pallas kernels for 0% -> 0%
where the time goes in v1:
time: 50.8 us; the launch traced here: 50.4 us
  Pallas kernels  39.1 us (77%)
  local copies, waits for them, and re-layouts  10.6 us (21%)
  between operations  0.66 us (1%)
    pallas_call x1, Pallas kernels, local(): pl.pallas_call(functools.partial(kernel, n_ctx, n_dp, reduce_here), out_s...  39.1 us
    unnamed x20, local copies, waits for them, and re-layouts  10.6 us

profile of v1, /device:TPU:0, one launch (start us, length us, event | category | flops | bytes accessed | tf_op | source)
XLA Modules:
  0.0 50.4 jit_solution(16586023276070568776)
XLA Ops:
  0.6 0.0 copy-start
  0.6 1.6 %copy-done = bf16[1,256,4096]{2,1,0:T(8,128)(2,1)S(1)} copy-done((bf16[1,256,4096]{2,1,0:T(8,128)(2,1)S(1)}, bf16[1,256,4096]{2,1,0:T(8,128)(2,1)}, u32[]{:S(2)}) %copy-start) | copy-done | bytes 2097176
  2.2 0.0 copy-start.1
  2.2 1.0 %copy-done.1 = bf16[1,256,1024]{2,1,0:T(8,128)(2,1)S(1)} copy-done((bf16[1,256,1024]{2,1,0:T(8,128)(2,1)S(1)}, bf16[1,256,1024]{2,1,0:T(8,128)(2,1)}, u32[]{:S(2)}) %copy-start.1) | copy-done | bytes 524312
  3.3 0.0 copy-start.2
  3.3 1.0 %copy-done.2 = bf16[1,256,1024]{2,1,0:T(8,128)(2,1)S(1)} copy-done((bf16[1,256,1024]{2,1,0:T(8,128)(2,1)S(1)}, bf16[1,256,1024]{2,1,0:T(8,128)(2,1)}, u32[]{:S(2)}) %copy-start.2) | copy-done | bytes 524312
  4.3 0.0 copy-start.3
  4.3 1.0 %copy-done.3 = bf16[1,256,1024]{2,1,0:T(8,128)(2,1)S(1)} copy-done((bf16[1,256,1024]{2,1,0:T(8,128)(2,1)S(1)}, bf16[1,256,1024]{2,1,0:T(8,128)(2,1)}, u32[]{:S(2)}) %copy-start.3) | copy-done | bytes 524312
  5.4 0.0 copy-start.4
  5.4 0.8 %copy-done.4 = bf16[1,256,128]{2,1,0:T(8,128)(2,1)S(1)} copy-done((bf16[1,256,128]{2,1,0:T(8,128)(2,1)S(1)}, bf16[1,256,128]{2,1,0:T(8,128)(2,1)}, u32[]{:S(2)}) %copy-start.4) | copy-done | bytes 65560
  6.2 0.0 copy-start.5
  6.2 0.8 %copy-done.5 = bf16[1,256,128]{2,1,0:T(8,128)(2,1)S(1)} copy-done((bf16[1,256,128]{2,1,0:T(8,128)(2,1)S(1)}, bf16[1,256,128]{2,1,0:T(8,128)(2,1)}, u32[]{:S(2)}) %copy-start.5) | copy-done | bytes 65560
  7.0 0.0 copy-start.6
  7.0 0.7 %copy-done.6 = f32[1,8,256]{2,1,0:T(8,128)S(1)} copy-done((f32[1,8,256]{2,1,0:T(8,128)S(1)}, f32[1,8,256]{2,1,0:T(8,128)}, u32[]{:S(2)}) %copy-start.6) | copy-done | bytes 8216
  7.7 0.0 copy-start.7
  7.7 0.7 %copy-done.7 = s32[1,256]{1,0:T(1,128)S(1)} copy-done((s32[1,256]{1,0:T(1,128)S(1)}, s32[1,256]{1,0:T(1,128)}, u32[]{:S(2)}) %copy-start.7) | copy-done | bytes 1048
  8.4 39.1 %shard_map.111 = (bf16[1,256,1024]{2,1,0:T(8,128)(2,1)S(1)}, bf16[1,256,128]{2,1,0:T(8,128)(2,1)S(1)}, bf16[1,256,128]{2,1,0:T(8,128)(2,1)S(1)}, f32[1024,128]{1,0:T(8,128)S(1)}) custom-call(bf16[1,256,1024]{2,1,0:T(8,128)(2,1)S(1)} %copy-done.1, bf16[1,256,128]{2,1,0:T(8,128)(2,1)S(1)} %copy-done.4, bf16[1,256,128]{2,1,0:T(8,128)(2,1)S(1)} %copy-done.5, ...), custom_call_target="tpu_custom_call" | custom-call | tf_op jit(solution)/shard_map/pallas_call | solution.py:304
  47.5 0.8 %copy.16 = bf16[1,256,1024]{2,1,0:T(8,128)(2,1)} copy(bf16[1,256,1024]{2,1,0:T(8,128)(2,1)S(1)} %get-tuple-element.8) | data formatting | bytes 1048576
  48.3 0.6 %copy.17 = bf16[1,256,128]{2,1,0:T(8,128)(2,1)} copy(bf16[1,256,128]{2,1,0:T(8,128)(2,1)S(1)} %get-tuple-element.9) | data formatting | bytes 131072
  49.0 0.6 %copy.18 = bf16[1,256,128]{2,1,0:T(8,128)(2,1)} copy(bf16[1,256,128]{2,1,0:T(8,128)(2,1)S(1)} %get-tuple-element.10) | data formatting | bytes 131072
  49.6 0.8 %copy.19 = f32[1024,128]{1,0:T(8,128)} copy(f32[1024,128]{1,0:T(8,128)S(1)} %get-tuple-element.11) | data formatting | bytes 1048576
Async XLA Ops:
  0.6 1.6 %copy-start = (bf16[1,256,4096]{2,1,0:T(8,128)(2,1)S(1)}, bf16[1,256,4096]{2,1,0:T(8,128)(2,1)}, u32[]{:S(2)}) copy-start(bf16[1,256,4096]{2,1,0:T(8,128)(2,1)} %refs_7_.1) | copy-start | bytes 6291460
  2.2 1.0 %copy-start.1 = (bf16[1,256,1024]{2,1,0:T(8,128)(2,1)S(1)}, bf16[1,256,1024]{2,1,0:T(8,128)(2,1)}, u32[]{:S(2)}) copy-start(bf16[1,256,1024]{2,1,0:T(8,128)(2,1)} %refs_0_.1) | copy-start | bytes 1572868
  3.3 1.0 %copy-start.2 = (bf16[1,256,1024]{2,1,0:T(8,128)(2,1)S(1)}, bf16[1,256,1024]{2,1,0:T(8,128)(2,1)}, u32[]{:S(2)}) copy-start(bf16[1,256,1024]{2,1,0:T(8,128)(2,1)} %refs_3_.1) | copy-start | bytes 1572868
  4.3 1.0 %copy-start.3 = (bf16[1,256,1024]{2,1,0:T(8,128)(2,1)S(1)}, bf16[1,256,1024]{2,1,0:T(8,128)(2,1)}, u32[]{:S(2)}) copy-start(bf16[1,256,1024]{2,1,0:T(8,128)(2,1)} %refs_4_.1) | copy-start | bytes 1572868
  5.4 0.8 %copy-start.4 = (bf16[1,256,128]{2,1,0:T(8,128)(2,1)S(1)}, bf16[1,256,128]{2,1,0:T(8,128)(2,1)}, u32[]{:S(2)}) copy-start(bf16[1,256,128]{2,1,0:T(8,128)(2,1)} %refs_1_.1) | copy-start | bytes 196612
  6.2 0.8 %copy-start.5 = (bf16[1,256,128]{2,1,0:T(8,128)(2,1)S(1)}, bf16[1,256,128]{2,1,0:T(8,128)(2,1)}, u32[]{:S(2)}) copy-start(bf16[1,256,128]{2,1,0:T(8,128)(2,1)} %refs_2_.1) | copy-start | bytes 196612
  7.0 0.7 %copy-start.6 = (f32[1,8,256]{2,1,0:T(8,128)S(1)}, f32[1,8,256]{2,1,0:T(8,128)}, u32[]{:S(2)}) copy-start(f32[1,8,256]{2,1,0:T(8,128)} %refs_5_.1) | copy-start | bytes 24580
  7.7 0.7 %copy-start.7 = (s32[1,256]{1,0:T(1,128)S(1)}, s32[1,256]{1,0:T(1,128)}, u32[]{:S(2)}) copy-start(s32[1,256]{1,0:T(1,128)} %refs_6_.1) | copy-start | bytes 3076

commit v2 on v1

v2 whole, which is shorter than its diff:
```python
import functools

import jax
import jax.numpy as jnp
from jax import lax
from jax.experimental import pallas as pl
from jax.experimental.pallas import tpu as pltpu
from jax.sharding import PartitionSpec as P

QH = 8
WINDOW = 256
F32 = jnp.float32
BF16 = jnp.bfloat16
NT = (((1,), (1,)), ((), ()))


def dot(a, b):
    return jnp.dot(a, b, preferred_element_type=F32)


def dot_nt(a, b):
    return lax.dot_general(a, b, NT, preferred_element_type=F32)


def remote(src, dst, send, recv, where):
    return pltpu.make_async_remote_copy(
        src_ref=src, dst_ref=dst, send_sem=send, recv_sem=recv,
        device_id=where, device_id_type=pl.DeviceIdType.MESH,
    )


def kernel(n_ctx, n_dp, reduce_here, *refs):
    (q_in, k_in, v_in, o_in, g_in, lse_in, start_in, x_in) = refs[:8]
    n_out = 4 if reduce_here else 3
    outs = refs[8:8 + n_out]
    dq_out, dk_out, dv_out = outs[:3]
    scratch = refs[8 + n_out:]
    (q, k, v, o, g, lse, start, delta, kp, vp, ds_all, dq, dk_own, dv_own, dk_near, dv_near,
     dk_send, dv_send, dk_back, dv_back, dk_low, dv_low, load, store, halo_s, halo_r, back_s, back_r) = scratch[:28]
    rows, width = q.shape
    head = width // QH
    scale = head ** (-0.5)
    c = lax.axis_index("ctx")
    d = lax.axis_index("dp")
    after = lax.rem(c + 1, n_ctx)
    before = lax.rem(c + n_ctx - 1, n_ctx)

    loads = [
        pltpu.make_async_copy(src.at[0], dst, load.at[i])
        for i, (src, dst) in enumerate(
            ((k_in, k), (v_in, v), (q_in, q), (g_in, g), (o_in, o), (lse_in, lse))
        )
    ]
    loads.append(pltpu.make_async_copy(start_in, start, load.at[6]))
    for copy in loads:
        copy.start()

    partners = [(after, d), (before, d)]
    if reduce_here:
        (tot_out,) = outs[3:]
        (xl, xr, dkt, dkt_r, wf, s1, r1, s2, r2, s3, r3, gb,
         xload, x_s, x_r, t_s, t_r, p1_s, p1_r, p2_s, p2_r, p3_s, p3_r, ag_s, ag_r) = scratch[28:]
        nz = n_ctx // 2
        block = x_in.shape[2] // n_dp
        core, y = lax.rem(d, 2), d // 2
        xx, z = lax.rem(c, 2), c // 2
        at_core = (c, y * 2 + 1 - core)
        at_y = (c, (1 - y) * 2 + core)
        at_x = (z * 2 + 1 - xx, d)
        at_z = [(lax.rem(z + s + 1, nz) * 2 + xx, d) for s in range(nz - 1)]
        partners += [at_core, at_y, at_x] + at_z
    barrier = pltpu.get_barrier_semaphore()
    for where in partners:
        pl.semaphore_signal(barrier, inc=1, device_id=where, device_id_type=pl.DeviceIdType.MESH)
    pl.semaphore_wait(barrier, len(partners))

    halo = [
        remote(src.at[0], dst, halo_s.at[i], halo_r.at[i], (after, d))
        for i, (src, dst) in enumerate(((k_in, kp), (v_in, vp)))
    ]
    for copy in halo:
        copy.start()
    for copy in loads:
        copy.wait()
    lane = lax.broadcasted_iota(jnp.int32, (rows, 128), 1)
    spread = jnp.zeros((rows, 128), F32)
    for h in range(QH):
        cols = slice(h * head, (h + 1) * head)
        one = jnp.sum(g[:, cols].astype(F32) * o[:, cols].astype(F32), axis=1, keepdims=True)
        spread = jnp.where(lane == h, one, spread)
    delta[...] = spread.T[:QH]

    s_at = lax.broadcasted_iota(jnp.int32, (rows, rows), 0)
    t_at = lax.broadcasted_iota(jnp.int32, (rows, rows), 1)
    first = start[...] - c * rows

    def part(keys, values, allowed, base, dk_sum, dv_sum):
        def one(h):
            cols = slice(h * head, (h + 1) * head)
            qh, gh = q[:, cols], g[:, cols]
            s = dot_nt(keys[...], qh)
            dp = dot_nt(values[...], gh)
            p = jnp.where(allowed, jnp.exp(s * scale - lse[h:h + 1, :]), 0.0)
            low = p.astype(BF16)
            sg = (p * (dp - delta[h:h + 1, :]) * scale).astype(BF16)
            ds_all[h, base:base + rows, :] = sg
            return dot(sg, qh), dot(low, gh)

        def body(i, carry):
            a, b = one(2 * i), one(2 * i + 1)
            dk_sum[...] += a[0] + b[0]
            dv_sum[...] += a[1] + b[1]
            return carry

        dk_sum[...] = jnp.zeros_like(dk_sum)
        dv_sum[...] = jnp.zeros_like(dv_sum)
        for i in range(QH // 2):
            body(i, 0)

    part(k, v, (s_at >= first) & (s_at <= t_at), 0, dk_own, dv_own)
    for copy in halo:
        copy.wait()
    if reduce_here:
        xcopies = []
        for yy in range(2):
            mine = pl.ds(pl.multiple_of((yy * 2 + core) * block, block), block)
            other = pl.ds(pl.multiple_of((yy * 2 + 1 - core) * block, block), block)
            xcopies.append(pltpu.make_async_copy(x_in.at[0, :, mine], xl.at[yy], xload.at[yy]))
            xcopies.append(remote(x_in.at[0, :, other], xr.at[yy], x_s.at[yy], x_r.at[yy], at_core))
        for copy in xcopies:
            copy.start()

    part(kp, vp, (s_at - WINDOW >= first) & (t_at - s_at + WINDOW < WINDOW), rows, dk_near, dv_near)
    dk_send[...] = dk_near[...].astype(BF16)
    back = [
        remote(src, dst, back_s.at[i], back_r.at[i], (before, d))
        for i, (src, dst) in enumerate(((dk_send, dk_back), (dv_send, dv_back)))
    ]
    back[0].start()
    dv_send[...] = dv_near[...].astype(BF16)
    back[1].start()

    kt = jnp.concatenate([k[...].astype(F32).T, kp[...].astype(F32).T], axis=1).astype(BF16)

    def dq_heads(lo, hi):
        for h in range(lo, hi):
            cols = slice(h * head, (h + 1) * head)
            dq[:, cols] = dot(kt, ds_all[h]).T.astype(BF16)

    def finish_dq():
        dq_heads(QH // 2, QH)
        copy = pltpu.make_async_copy(dq, dq_out.at[0], store.at[0])
        copy.start()
        return copy

    dq_heads(0, QH // 2)

    back[0].wait()
    dk = dk_own[...] + dk_back[...].astype(F32)
    dk_low[...] = dk.astype(BF16)
    dk_store = pltpu.make_async_copy(dk_low, dk_out.at[0], store.at[1])

    if reduce_here:
        dkt[...] = dk.T.astype(BF16)
        trade = remote(dkt, dkt_r, t_s.at[0], t_r.at[0], at_core)
        trade.start()
    dk_store.start()

    def finish_dv():
        back[1].wait()
        dv_low[...] = (dv_own[...] + dv_back[...].astype(F32)).astype(BF16)
        copy = pltpu.make_async_copy(dv_low, dv_out.at[0], store.at[2])
        copy.start()
        return copy

    if reduce_here:
        for copy in xcopies:
            copy.wait()
        order = []
        for j in range(nz // 2):
            order += [j, nz - 1 - j]
        away = 1 - y

        def chunk(src, left, yy, j):
            return dot(left[...], src[yy, :, j * 256:(j + 1) * 256])

        for yy in (away, y):
            for j in order:
                got = chunk(xl, dkt, yy, j)
                wf[yy, 2 * j] = got[:, :128]
                wf[yy, 2 * j + 1] = got[:, 128:]
        trade.wait()

        over_y, over_x = {}, {}
        for j in order:
            got = chunk(xr, dkt_r, away, j)
            s1[j, 0] = (wf[away, 2 * j] + got[:, :128]).astype(BF16)
            s1[j, 1] = (wf[away, 2 * j + 1] + got[:, 128:]).astype(BF16)
            over_y[j] = remote(s1.at[j], r1.at[j], p1_s.at[j], p1_r.at[j], at_y)
            over_y[j].start()
        for j in order:
            got = chunk(xr, dkt_r, y, j)
            wf[y, 2 * j] += got[:, :128]
            wf[y, 2 * j + 1] += got[:, 128:]

        def step_x(j):
            over_y[j].wait_recv()
            s2[j] = (wf[y, 2 * j + 1 - xx] + r1[j, 1 - xx].astype(F32)).astype(BF16)
            over_x[j] = remote(s2.at[j], r2.at[j], p2_s.at[j], p2_r.at[j], at_x)
            over_x[j].start()

        def to_owner(j):
            return remote(s3.at[j], r3.at[z], p3_s.at[j], p3_r.at[z], (j * 2 + xx, d))

        def step_z(j):
            over_x[j].wait_recv()
            kept = wf[y, 2 * j + xx] + r1[j, xx].astype(F32) + r2[j].astype(F32)
            wf[y, 2 * j + xx] = kept
            s3[j] = kept.astype(BF16)

            @pl.when(z != j)
            def _():
                to_owner(j).start()

        def over_z(t):
            return remote(gb.at[c], gb.at[c], ag_s.at[t], ag_r.at[z], (t * 2 + xx, d))

        def pass_x(j):
            at = j * 2 + xx
            return remote(gb.at[at], gb.at[at], ag_s.at[nz + j], ag_r.at[nz + j], at_x)

        def step_own(j):
            @pl.when(z == j)
            def _():
                total = wf[y, 2 * j + xx]
                for t in range(nz):
                    if t != j:
                        remote(s3.at[t], r3.at[t], p3_s.at[t], p3_r.at[t], at_y).wait_recv()
                        total = total + r3[t].astype(F32)
                gb[2 * j + xx] = total.T.astype(BF16)
                for t in range(nz):
                    if t != j:
                        over_z(t).start()
                pass_x(j).start()

        dv_store = finish_dv()
        dq_store = finish_dq()
        for i in range(nz + 2):
            if i < nz:
                step_x(order[i])
            if 1 <= i <= nz:
                step_z(order[i - 1])
            if i >= 2:
                step_own(order[i - 2])
        for j in order:
            @pl.when(z != j)
            def _():
                at = j * 2 + xx
                remote(gb.at[at], gb.at[at], ag_s.at[j], ag_r.at[j], at_y).wait_recv()
                pass_x(j).start()
        for j in order:
            at = j * 2 + 1 - xx
            remote(gb.at[at], gb.at[at], ag_s.at[nz + j], ag_r.at[nz + j], at_x).wait_recv()
        tot_store = pltpu.make_async_copy(gb, tot_out, store.at[3])
        tot_store.start()
        for j in order:
            over_y[j].wait_send()
            over_x[j].wait_send()
            pass_x(j).wait_send()

            @pl.when(z != j)
            def _():
                to_owner(j).wait_send()
                over_z(j).wait_send()
        tot_store.wait()
    else:
        dv_store = finish_dv()
        dq_store = finish_dq()
    dq_store.wait()
    dk_store.wait()
    dv_store.wait()


def hand_over_kernel(count, *refs):
    arrays, outs, held = refs[:count], refs[count:2 * count], refs[2 * count:3 * count]
    wide, arrive, leave = refs[3 * count:]
    loads = [pltpu.make_async_copy(arrays[i], held[i], arrive.at[i]) for i in range(count)]
    stores = [pltpu.make_async_copy(held[i], outs[i], leave.at[i]) for i in range(count - 1)]
    stores.append(pltpu.make_async_copy(wide, outs[-1], leave.at[count - 1]))
    places = [count - 1] + list(range(count - 1))
    for i in places:
        loads[i].start()
    for i in places:
        loads[i].wait()
        if i == count - 1:
            wide[...] = held[i][...].astype(F32).reshape(wide.shape)
        stores[i].start()
    for copy in stores:
        copy.wait()


def hand_over(arrays):
    *same, last = arrays
    count = len(arrays)
    total = jax.ShapeDtypeStruct((last.shape[0] * last.shape[1], last.shape[2]), F32)
    return pl.pallas_call(
        functools.partial(hand_over_kernel, count),
        out_shape=[jax.ShapeDtypeStruct(a.shape, a.dtype) for a in same] + [total],
        in_specs=[pl.BlockSpec(memory_space=pl.ANY)] * count,
        out_specs=[pl.BlockSpec(memory_space=pltpu.HBM)] * count,
        scratch_shapes=[pltpu.VMEM(a.shape, a.dtype) for a in arrays]
        + [pltpu.VMEM(total.shape, F32), pltpu.SemaphoreType.DMA((count,)), pltpu.SemaphoreType.DMA((count,))],
    )(*arrays)


def local(n_ctx, n_dp, query, keys, values, attn_out, out_grad, lse, doc_start, inputs):
    _, rows, width = query.shape
    head = width // QH
    depth = inputs.shape[2]
    reduce_here = n_dp == 4 and n_ctx % 4 == 0 and depth == n_dp * n_ctx * 128 and head == 128
    nz = n_ctx // 2
    any_space = pl.BlockSpec(memory_space=pl.ANY)
    out_shape = [
        jax.ShapeDtypeStruct(query.shape, BF16),
        jax.ShapeDtypeStruct(keys.shape, BF16),
        jax.ShapeDtypeStruct(keys.shape, BF16),
    ]
    dma = pltpu.SemaphoreType.DMA
    small = pltpu.VMEM((rows, head), BF16)
    wide = pltpu.VMEM((rows, head), F32)
    full = pltpu.VMEM((rows, width), BF16)
    scratch = [
        full, small, small, full, full, pltpu.VMEM((QH, rows), F32), pltpu.VMEM((1, rows), jnp.int32),
        pltpu.VMEM((QH, rows), F32), small, small, pltpu.VMEM((QH, 2 * rows, rows), BF16), full,
        wide, wide, wide, wide, small, small, small, small, small, small,
        dma((7,)), dma((4,)), dma((2,)), dma((2,)), dma((2,)), dma((2,)),
    ]
    if reduce_here:
        out_shape.append(jax.ShapeDtypeStruct((n_ctx, 128, head), BF16))
        scratch += [
            pltpu.VMEM((2, rows, depth // n_dp), BF16), pltpu.VMEM((2, rows, depth // n_dp), BF16),
            pltpu.VMEM((head, rows), BF16), pltpu.VMEM((head, rows), BF16),
            pltpu.VMEM((2, n_ctx, 128, 128), F32),
            pltpu.VMEM((nz, 2, 128, 128), BF16), pltpu.VMEM((nz, 2, 128, 128), BF16),
            pltpu.VMEM((nz, 128, 128), BF16), pltpu.VMEM((nz, 128, 128), BF16),
            pltpu.VMEM((nz, 128, 128), BF16), pltpu.VMEM((nz, 128, 128), BF16),
            pltpu.VMEM((n_ctx, 128, 128), BF16),
            dma((2,)), dma((2,)), dma((2,)), dma((1,)), dma((1,)), dma((nz,)), dma((nz,)), dma((nz,)), dma((nz,)),
            dma((nz,)), dma((nz,)), dma((2 * nz,)), dma((2 * nz,)),
        ]
    got = pl.pallas_call(
        functools.partial(kernel, n_ctx, n_dp, reduce_here),
        out_shape=out_shape,
        in_specs=[pl.BlockSpec(memory_space=pltpu.HBM)] * 8,
        out_specs=[any_space] * len(out_shape),
        scratch_shapes=scratch,
        compiler_params=pltpu.CompilerParams(
            collective_id=0, has_side_effects=True, vmem_limit_bytes=56 * 1024 * 1024
        ),
    )(query, keys, values, attn_out, out_grad, lse, doc_start, inputs)
    if reduce_here:
        return tuple(hand_over(got))
    dq, dk, dv = got
    term = lax.dot_general(
        inputs[0], dk[0], (((0,), (0,)), ((), ())), preferred_element_type=jnp.float32
    )
    return dq, dk, dv, lax.psum(lax.psum_scatter(term, "dp", scatter_dimension=0, tiled=True), "ctx")


def solution(mesh):
    in_specs = (
        P("dp", "ctx", None),
        P("dp", "ctx", None),
        P("dp", "ctx", None),
        P("dp", "ctx", None),
        P("dp", "ctx", None),
        P("dp", None, "ctx"),
        P("dp", "ctx"),
        P("dp", "ctx", None),
    )
    out_specs = (P("dp", "ctx", None), P("dp", "ctx", None), P("dp", "ctx", None), P("dp", None))
    return jax.shard_map(
        functools.partial(local, mesh.shape["ctx"], mesh.shape["dp"]),
        mesh=mesh, in_specs=in_specs, out_specs=out_specs, check_vma=False,
    )
```

time: 50.8 us -> 46.7 us (0.919)
  local copies, waits for them, and re-layouts: 10.6 us -> 0 us
  Pallas kernels: 39.1 us -> 45.9 us
    unnamed x20 -> x0, local copies, waits for them, and re-layouts: 10.6 us -> none
    pallas_call x1, Pallas kernels: 39.1 us -> 43.8 us  [local(): pl.pallas_call(functools.partial(kernel, n_ctx, n_dp, reduce_here), out_s...]
    pallas_call x0 -> x1, Pallas kernels: none -> 2.05 us  [hand_over(): pl.pallas_call(functools.partial(hand_over_kernel, count), out_shape=[jax...]
where the time goes in v2:
time: 46.7 us; the launch traced here: 46.5 us
  Pallas kernels  45.9 us (98%)
  between operations  0.64 us (1%)
    pallas_call x1, Pallas kernels, local(): pl.pallas_call(functools.partial(kernel, n_ctx, n_dp, reduce_here), out_s...  43.8 us
    pallas_call x1, Pallas kernels, hand_over(): pl.pallas_call(functools.partial(hand_over_kernel, count), out_shape=[jax...  2.05 us

profile of v2, /device:TPU:0, one launch (start us, length us, event | category | flops | bytes accessed | tf_op | source)
XLA Modules:
  0.0 46.5 jit_solution(9490808153019848821)
XLA Ops:
  0.6 43.8 %shard_map.111 = (bf16[1,256,1024]{2,1,0:T(8,128)(2,1)}, bf16[1,256,128]{2,1,0:T(8,128)(2,1)}, bf16[1,256,128]{2,1,0:T(8,128)(2,1)}, bf16[8,128,128]{2,1,0:T(8,128)(2,1)}) custom-call(bf16[1,256,1024]{2,1,0:T(8,128)(2,1)} %refs_0_.1, bf16[1,256,128]{2,1,0:T(8,128)(2,1)} %refs_1_.1, bf16[1,256,128]{2,1,0:T(8,128)(2,1)} %refs_2_.1, ...), custom_call_target="tpu_custom_call" | custom-call | tf_op jit(solution)/shard_map/pallas_call | solution.py:351
  44.4 2.1 %shard_map.112 = (bf16[1,256,1024]{2,1,0:T(8,128)(2,1)}, bf16[1,256,128]{2,1,0:T(8,128)(2,1)}, bf16[1,256,128]{2,1,0:T(8,128)(2,1)}, f32[1024,128]{1,0:T(8,128)}) custom-call(bf16[1,256,1024]{2,1,0:T(8,128)(2,1)} %get-tuple-element.8.refs_0_, bf16[1,256,128]{2,1,0:T(8,128)(2,1)} %get-tuple-element.9.refs_1_, bf16[1,256,128]{2,1,0:T(8,128)(2,1)} %get-tuple-element.10.refs_2_, ...), custom_call_target="tpu_custom_call" | custom-call | tf_op jit(solution)/shard_map/pallas_call | solution.py:306

commit v3 on v2

--- a/solution.py
+++ b/solution.py
@@ -36,7 +36,7 @@
     dq_out, dk_out, dv_out = outs[:3]
     scratch = refs[8 + n_out:]
     (q, k, v, o, g, lse, start, delta, kp, vp, ds_all, dq, dk_own, dv_own, dk_near, dv_near,
-     dk_send, dv_send, dk_back, dv_back, dk_low, dv_low, load, store, halo_s, halo_r, back_s, back_r) = scratch[:28]
+     dk_send, dv_send, dk_back, dv_back, dk_low, dv_low, load, store, halo_s, halo_r, back_s, back_r, probs) = scratch[:29]
     rows, width = q.shape
     head = width // QH
     scale = head ** (-0.5)
@@ -58,17 +58,18 @@
     partners = [(after, d), (before, d)]
     if reduce_here:
         (tot_out,) = outs[3:]
-        (xl, xr, dkt, dkt_r, wf, s1, r1, s2, r2, s3, r3, gb,
-         xload, x_s, x_r, t_s, t_r, p1_s, p1_r, p2_s, p2_r, p3_s, p3_r, ag_s, ag_r) = scratch[28:]
+        (xl, xr, dkt, dkt_r, wf, s1, r1, s2, r2, gb,
+         xload, x_s, x_r, t_s, t_r, p1_s, p1_r, p2_s, p2_r, ag_s, ag_r) = scratch[29:]
         nz = n_ctx // 2
         block = x_in.shape[2] // n_dp
         core, y = lax.rem(d, 2), d // 2
         xx, z = lax.rem(c, 2), c // 2
         at_core = (c, y * 2 + 1 - core)
         at_y = (c, (1 - y) * 2 + core)
-        at_x = (z * 2 + 1 - xx, d)
-        at_z = [(lax.rem(z + s + 1, nz) * 2 + xx, d) for s in range(nz - 1)]
-        partners += [at_core, at_y, at_x] + at_z
+        far = [(s, e) for s in range(1, nz) for e in (0, 1)] + [(0, 1)]
+        at = {(s, e): (lax.rem(z + s, nz) * 2 + (1 - xx if e else xx), d) for s, e in far}
+        at_x = at[0, 1]
+        partners += [at_core, at_y] + [at[one] for one in far]
     barrier = pltpu.get_barrier_semaphore()
     for where in partners:
         pl.semaphore_signal(barrier, inc=1, device_id=where, device_id_type=pl.DeviceIdType.MESH)
@@ -80,6 +81,16 @@
     ]
     for copy in halo:
         copy.start()
+    if reduce_here:
+        xcopies = []
+        for yy in range(2):
+            mine = pl.ds(pl.multiple_of((yy * 2 + core) * block, block), block)
+            other = pl.ds(pl.multiple_of((yy * 2 + 1 - core) * block, block), block)
+            xcopies.append(pltpu.make_async_copy(x_in.at[0, :, mine], xl.at[yy], xload.at[yy]))
+            xcopies.append(remote(x_in.at[0, :, other], xr.at[yy], x_s.at[yy], x_r.at[yy], at_core))
+        for copy in xcopies:
+            copy.start()
+
     for copy in loads:
         copy.wait()
     lane = lax.broadcasted_iota(jnp.int32, (rows, 128), 1)
@@ -118,19 +129,23 @@
             body(i, 0)
 
     part(k, v, (s_at >= first) & (s_at <= t_at), 0, dk_own, dv_own)
-    for copy in halo:
-        copy.wait()
-    if reduce_here:
-        xcopies = []
-        for yy in range(2):
-            mine = pl.ds(pl.multiple_of((yy * 2 + core) * block, block), block)
-            other = pl.ds(pl.multiple_of((yy * 2 + 1 - core) * block, block), block)
-            xcopies.append(pltpu.make_async_copy(x_in.at[0, :, mine], xl.at[yy], xload.at[yy]))
-            xcopies.append(remote(x_in.at[0, :, other], xr.at[yy], x_s.at[yy], x_r.at[yy], at_core))
-        for copy in xcopies:
-            copy.start()
-
-    part(kp, vp, (s_at - WINDOW >= first) & (t_at - s_at + WINDOW < WINDOW), rows, dk_near, dv_near)
+    near = (s_at - WINDOW >= first) & (t_at - s_at + WINDOW < WINDOW)
+    halo[0].wait()
+    for h in range(QH):
+        cols = slice(h * head, (h + 1) * head)
+        score = dot_nt(kp[...], q[:, cols]) * scale - lse[h:h + 1, :]
+        p = jnp.where(near, jnp.exp(score), 0.0)
+        probs[h] = p
+        term = dot(p.astype(BF16), g[:, cols])
+        dv_near[...] = term if h == 0 else dv_near[...] + term
+    halo[1].wait()
+    for h in range(QH):
+        cols = slice(h * head, (h + 1) * head)
+        dp = dot_nt(vp[...], g[:, cols])
+        sg = (probs[h] * (dp - delta[h:h + 1, :]) * scale).astype(BF16)
+        ds_all[h, rows:, :] = sg
+        term = dot(sg, q[:, cols])
+        dk_near[...] = term if h == 0 else dk_near[...] + term
     dk_send[...] = dk_near[...].astype(BF16)
     back = [
         remote(src, dst, back_s.at[i], back_r.at[i], (before, d))
@@ -176,102 +191,70 @@
     if reduce_here:
         for copy in xcopies:
             copy.wait()
-        order = []
-        for j in range(nz // 2):
-            order += [j, nz - 1 - j]
-        away = 1 - y
-
-        def chunk(src, left, yy, j):
-            return dot(left[...], src[yy, :, j * 256:(j + 1) * 256])
-
-        for yy in (away, y):
-            for j in order:
-                got = chunk(xl, dkt, yy, j)
-                wf[yy, 2 * j] = got[:, :128]
-                wf[yy, 2 * j + 1] = got[:, 128:]
+        steps = list(range(1, nz)) + [0]
+        places = [lax.rem(z + s, nz) for s in range(nz)]
+
+        def chunk(src, left, yy, s):
+            cols = pl.ds(pl.multiple_of(places[s] * 256, 256), 256)
+            return dot(left[...], src[yy, :, cols])
+
+        for yy in (1 - y, y):
+            for s in steps:
+                got = chunk(xl, dkt, yy, s)
+                wf[yy, 2 * s] = got[:, :128]
+                wf[yy, 2 * s + 1] = got[:, 128:]
         trade.wait()
 
-        over_y, over_x = {}, {}
-        for j in order:
-            got = chunk(xr, dkt_r, away, j)
-            s1[j, 0] = (wf[away, 2 * j] + got[:, :128]).astype(BF16)
-            s1[j, 1] = (wf[away, 2 * j + 1] + got[:, 128:]).astype(BF16)
-            over_y[j] = remote(s1.at[j], r1.at[j], p1_s.at[j], p1_r.at[j], at_y)
-            over_y[j].start()
-        for j in order:
-            got = chunk(xr, dkt_r, y, j)
-            wf[y, 2 * j] += got[:, :128]
-            wf[y, 2 * j + 1] += got[:, 128:]
-
-        def step_x(j):
-            over_y[j].wait_recv()
-            s2[j] = (wf[y, 2 * j + 1 - xx] + r1[j, 1 - xx].astype(F32)).astype(BF16)
-            over_x[j] = remote(s2.at[j], r2.at[j], p2_s.at[j], p2_r.at[j], at_x)
-            over_x[j].start()
-
-        def to_owner(j):
-            return remote(s3.at[j], r3.at[z], p3_s.at[j], p3_r.at[z], (j * 2 + xx, d))
-
-        def step_z(j):
-            over_x[j].wait_recv()
-            kept = wf[y, 2 * j + xx] + r1[j, xx].astype(F32) + r2[j].astype(F32)
-            wf[y, 2 * j + xx] = kept
-            s3[j] = kept.astype(BF16)
-
-            @pl.when(z != j)
-            def _():
-                to_owner(j).start()
-
-        def over_z(t):
-            return remote(gb.at[c], gb.at[c], ag_s.at[t], ag_r.at[z], (t * 2 + xx, d))
-
-        def pass_x(j):
-            at = j * 2 + xx
-            return remote(gb.at[at], gb.at[at], ag_s.at[nz + j], ag_r.at[nz + j], at_x)
-
-        def step_own(j):
-            @pl.when(z == j)
-            def _():
-                total = wf[y, 2 * j + xx]
-                for t in range(nz):
-                    if t != j:
-                        remote(s3.at[t], r3.at[t], p3_s.at[t], p3_r.at[t], at_y).wait_recv()
-                        total = total + r3[t].astype(F32)
-                gb[2 * j + xx] = total.T.astype(BF16)
-                for t in range(nz):
-                    if t != j:
-                        over_z(t).start()
-                pass_x(j).start()
-
+        over_y = {}
+        for s in steps:
+            got = chunk(xr, dkt_r, 1 - y, s)
+            s1[s, 0] = (wf[1 - y, 2 * s] + got[:, :128]).astype(BF16)
+            s1[s, 1] = (wf[1 - y, 2 * s + 1] + got[:, 128:]).astype(BF16)
+            over_y[s] = remote(s1.at[s], r1.at[s], p1_s.at[s], p1_r.at[s], at_y)
+            over_y[s].start()
+        for s in steps:
+            got = chunk(xr, dkt_r, y, s)
+            wf[y, 2 * s] += got[:, :128]
+            wf[y, 2 * s + 1] += got[:, 128:]
         dv_store = finish_dv()
         dq_store = finish_dq()
-        for i in range(nz + 2):
-            if i < nz:
-                step_x(order[i])
-            if 1 <= i <= nz:
-                step_z(order[i - 1])
-            if i >= 2:
-                step_own(order[i - 2])
-        for j in order:
-            @pl.when(z != j)
-            def _():
-                at = j * 2 + xx
-                remote(gb.at[at], gb.at[at], ag_s.at[j], ag_r.at[j], at_y).wait_recv()
-                pass_x(j).start()
-        for j in order:
-            at = j * 2 + 1 - xx
-            remote(gb.at[at], gb.at[at], ag_s.at[nz + j], ag_r.at[nz + j], at_x).wait_recv()
+
+        out = {}
+        for s in steps:
+            over_y[s].wait_recv()
+            for e in (0, 1):
+                half = 1 - xx if e else xx
+                piece = wf[y, 2 * s + half] + r1[s, half].astype(F32)
+                if (s, e) == (0, 0):
+                    total = piece
+                    continue
+                n = 2 * s + e
+                s2[n] = piece.astype(BF16)
+                out[s, e] = remote(s2.at[n], r2.at[n], p2_s.at[n], p2_r.at[n], at[s, e])
+                out[s, e].start()
+        for s, e in far:
+            out[s, e].wait_recv()
+            total = total + r2[2 * s + e].astype(F32)
+        gb[c] = total.T.astype(BF16)
+
+        over_z = [
+            remote(gb.at[c], gb.at[c], ag_s.at[s], ag_r.at[s], at[s, 0]) for s in range(1, nz)
+        ]
+        over_x = [remote(gb.at[c], gb.at[c], ag_s.at[nz], ag_r.at[nz], at_x)]
+        for copy in over_z + over_x:
+            copy.start()
+        for s in range(1, nz):
+            over_z[s - 1].wait_recv()
+            slot = lax.rem(z - s + nz, nz) * 2 + xx
+            copy = remote(gb.at[slot], gb.at[slot], ag_s.at[nz + s], ag_r.at[nz + s], at_x)
+            copy.start()
+            over_x.append(copy)
+        for copy in over_x:
+            copy.wait_recv()
         tot_store = pltpu.make_async_copy(gb, tot_out, store.at[3])
         tot_store.start()
-        for j in order:
-            over_y[j].wait_send()
-            over_x[j].wait_send()
-            pass_x(j).wait_send()
-
-            @pl.when(z != j)
-            def _():
-                to_owner(j).wait_send()
-                over_z(j).wait_send()
+        for copy in list(over_y.values()) + list(out.values()) + over_z + over_x:
+            copy.wait_send()
         tot_store.wait()
     else:
         dv_store = finish_dv()
@@ -334,6 +317,7 @@
         pltpu.VMEM((QH, rows), F32), small, small, pltpu.VMEM((QH, 2 * rows, rows), BF16), full,
         wide, wide, wide, wide, small, small, small, small, small, small,
         dma((7,)), dma((4,)), dma((2,)), dma((2,)), dma((2,)), dma((2,)),
+        pltpu.VMEM((QH, rows, rows), F32),
     ]
     if reduce_here:
         out_shape.append(jax.ShapeDtypeStruct((n_ctx, 128, head), BF16))
@@ -342,11 +326,10 @@
             pltpu.VMEM((head, rows), BF16), pltpu.VMEM((head, rows), BF16),
             pltpu.VMEM((2, n_ctx, 128, 128), F32),
             pltpu.VMEM((nz, 2, 128, 128), BF16), pltpu.VMEM((nz, 2, 128, 128), BF16),
-            pltpu.VMEM((nz, 128, 128), BF16), pltpu.VMEM((nz, 128, 128), BF16),
-            pltpu.VMEM((nz, 128, 128), BF16), pltpu.VMEM((nz, 128, 128), BF16),
+            pltpu.VMEM((n_ctx, 128, 128), BF16), pltpu.VMEM((n_ctx, 128, 128), BF16),
             pltpu.VMEM((n_ctx, 128, 128), BF16),
-            dma((2,)), dma((2,)), dma((2,)), dma((1,)), dma((1,)), dma((nz,)), dma((nz,)), dma((nz,)), dma((nz,)),
-            dma((nz,)), dma((nz,)), dma((2 * nz,)), dma((2 * nz,)),
+            dma((2,)), dma((2,)), dma((2,)), dma((1,)), dma((1,)), dma((nz,)), dma((nz,)), dma((n_ctx,)), dma((n_ctx,)),
+            dma((2 * nz,)), dma((2 * nz,)),
         ]
     got = pl.pallas_call(
         functools.partial(kernel, n_ctx, n_dp, reduce_here),

time: 46.7 us -> 40 us (0.86)
  Pallas kernels: 45.9 us -> 39.2 us
    pallas_call x1, Pallas kernels: 43.8 us -> 37.1 us  [local(): pl.pallas_call(functools.partial(kernel, n_ctx, n_dp, reduce_here), out_s...]
where the time goes in v3:
time: 40 us; the launch traced here: 39.8 us
  Pallas kernels  39.2 us (98%)
  between operations  0.64 us (2%)
    pallas_call x1, Pallas kernels, local(): pl.pallas_call(functools.partial(kernel, n_ctx, n_dp, reduce_here), out_s...  37.1 us
    pallas_call x1, Pallas kernels, hand_over(): pl.pallas_call(functools.partial(hand_over_kernel, count), out_shape=[jax...  2.05 us

profile of v3, /device:TPU:0, one launch (start us, length us, event | category | flops | bytes accessed | tf_op | source)
XLA Modules:
  0.0 39.8 jit_solution(8989874172153562596)
XLA Ops:
  0.6 37.1 %shard_map.111 = (bf16[1,256,1024]{2,1,0:T(8,128)(2,1)}, bf16[1,256,128]{2,1,0:T(8,128)(2,1)}, bf16[1,256,128]{2,1,0:T(8,128)(2,1)}, bf16[8,128,128]{2,1,0:T(8,128)(2,1)}) custom-call(bf16[1,256,1024]{2,1,0:T(8,128)(2,1)} %refs_0_.1, bf16[1,256,128]{2,1,0:T(8,128)(2,1)} %refs_1_.1, bf16[1,256,128]{2,1,0:T(8,128)(2,1)} %refs_2_.1, ...), custom_call_target="tpu_custom_call" | custom-call | tf_op jit(solution)/shard_map/pallas_call | solution.py:334
  37.8 2.1 %shard_map.112 = (bf16[1,256,1024]{2,1,0:T(8,128)(2,1)}, bf16[1,256,128]{2,1,0:T(8,128)(2,1)}, bf16[1,256,128]{2,1,0:T(8,128)(2,1)}, f32[1024,128]{1,0:T(8,128)}) custom-call(bf16[1,256,1024]{2,1,0:T(8,128)(2,1)} %get-tuple-element.8.refs_0_, bf16[1,256,128]{2,1,0:T(8,128)(2,1)} %get-tuple-element.9.refs_1_, bf16[1,256,128]{2,1,0:T(8,128)(2,1)} %get-tuple-element.10.refs_2_, ...), custom_call_target="tpu_custom_call" | custom-call | tf_op jit(solution)/shard_map/pallas_call | solution.py:289

commit v4 on v3

--- a/solution.py
+++ b/solution.py
@@ -58,8 +58,8 @@
     partners = [(after, d), (before, d)]
     if reduce_here:
         (tot_out,) = outs[3:]
-        (xl, xr, dkt, dkt_r, wf, s1, r1, s2, r2, gb,
-         xload, x_s, x_r, t_s, t_r, p1_s, p1_r, p2_s, p2_r, ag_s, ag_r) = scratch[29:]
+        (xl, xr, dkt, dkt_r, wf, s1, r1, s2, r2, s3, r3, gb,
+         xload, x_s, x_r, t_s, t_r, p1_s, p1_r, p2_s, p2_r, p3_s, p3_r, ag_s, ag_r) = scratch[29:]
         nz = n_ctx // 2
         block = x_in.shape[2] // n_dp
         core, y = lax.rem(d, 2), d // 2
@@ -205,34 +205,56 @@
                 wf[yy, 2 * s + 1] = got[:, 128:]
         trade.wait()
 
-        over_y = {}
+        def add(yy, s):
+            got = chunk(xr, dkt_r, yy, s)
+            wf[yy, 2 * s] += got[:, :128]
+            wf[yy, 2 * s + 1] += got[:, 128:]
+
+        first_out, second_out, out = {}, {}, {}
         for s in steps:
-            got = chunk(xr, dkt_r, 1 - y, s)
-            s1[s, 0] = (wf[1 - y, 2 * s] + got[:, :128]).astype(BF16)
-            s1[s, 1] = (wf[1 - y, 2 * s + 1] + got[:, 128:]).astype(BF16)
-            over_y[s] = remote(s1.at[s], r1.at[s], p1_s.at[s], p1_r.at[s], at_y)
-            over_y[s].start()
+            add(1 - y, s)
+            if s % 2:
+                s1[s, 0] = wf[1 - y, 2 * s].astype(BF16)
+                s1[s, 1] = wf[1 - y, 2 * s + 1].astype(BF16)
+            else:
+                add(y, s)
+                s1[s, 0] = wf[0, 2 * s + 1 - xx].astype(BF16)
+                s1[s, 1] = wf[1, 2 * s + 1 - xx].astype(BF16)
+            first_out[s] = remote(
+                s1.at[s], r1.at[s], p1_s.at[s], p1_r.at[s], at_y if s % 2 else at_x
+            )
+            first_out[s].start()
         for s in steps:
-            got = chunk(xr, dkt_r, y, s)
-            wf[y, 2 * s] += got[:, :128]
-            wf[y, 2 * s + 1] += got[:, 128:]
+            if s % 2:
+                add(y, s)
+
+        def to_owner(s, e, piece):
+            n = 2 * s + e
+            s2[n] = piece.astype(BF16)
+            out[s, e] = remote(s2.at[n], r2.at[n], p2_s.at[n], p2_r.at[n], at[s, e])
+            out[s, e].start()
+
+        for s in steps:
+            first_out[s].wait_recv()
+            if s % 2:
+                for e in (0, 1):
+                    half = 1 - xx if e else xx
+                    to_owner(s, e, wf[y, 2 * s + half] + r1[s, half].astype(F32))
+            else:
+                s3[s] = (wf[1 - y, 2 * s + xx] + r1[s, 1 - y].astype(F32)).astype(BF16)
+                second_out[s] = remote(s3.at[s], r3.at[s], p3_s.at[s], p3_r.at[s], at_y)
+                second_out[s].start()
+        for s in steps:
+            if s % 2 == 0:
+                second_out[s].wait_recv()
+                piece = wf[y, 2 * s + xx] + r1[s, y].astype(F32) + r3[s].astype(F32)
+                if s:
+                    to_owner(s, 0, piece)
+                else:
+                    total = piece
         dv_store = finish_dv()
         dq_store = finish_dq()
-
-        out = {}
-        for s in steps:
-            over_y[s].wait_recv()
-            for e in (0, 1):
-                half = 1 - xx if e else xx
-                piece = wf[y, 2 * s + half] + r1[s, half].astype(F32)
-                if (s, e) == (0, 0):
-                    total = piece
-                    continue
-                n = 2 * s + e
-                s2[n] = piece.astype(BF16)
-                out[s, e] = remote(s2.at[n], r2.at[n], p2_s.at[n], p2_r.at[n], at[s, e])
-                out[s, e].start()
-        for s, e in far:
+        for s, e in out:
             out[s, e].wait_recv()
             total = total + r2[2 * s + e].astype(F32)
         gb[c] = total.T.astype(BF16)
@@ -253,7 +275,7 @@
             copy.wait_recv()
         tot_store = pltpu.make_async_copy(gb, tot_out, store.at[3])
         tot_store.start()
-        for copy in list(over_y.values()) + list(out.values()) + over_z + over_x:
+        for copy in [*first_out.values(), *second_out.values(), *out.values()] + over_z + over_x:
             copy.wait_send()
         tot_store.wait()
     else:
@@ -300,7 +322,7 @@
     _, rows, width = query.shape
     head = width // QH
     depth = inputs.shape[2]
-    reduce_here = n_dp == 4 and n_ctx % 4 == 0 and depth == n_dp * n_ctx * 128 and head == 128
+    reduce_here = n_dp == 4 and n_ctx % 4 == 0 and rows == WINDOW and depth == n_dp * n_ctx * 128 and head == 128
     nz = n_ctx // 2
     any_space = pl.BlockSpec(memory_space=pl.ANY)
     out_shape = [
@@ -327,9 +349,10 @@
             pltpu.VMEM((2, n_ctx, 128, 128), F32),
             pltpu.VMEM((nz, 2, 128, 128), BF16), pltpu.VMEM((nz, 2, 128, 128), BF16),
             pltpu.VMEM((n_ctx, 128, 128), BF16), pltpu.VMEM((n_ctx, 128, 128), BF16),
+            pltpu.VMEM((nz, 128, 128), BF16), pltpu.VMEM((nz, 128, 128), BF16),
             pltpu.VMEM((n_ctx, 128, 128), BF16),
             dma((2,)), dma((2,)), dma((2,)), dma((1,)), dma((1,)), dma((nz,)), dma((nz,)), dma((n_ctx,)), dma((n_ctx,)),
-            dma((2 * nz,)), dma((2 * nz,)),
+            dma((nz,)), dma((nz,)), dma((2 * nz,)), dma((2 * nz,)),
         ]
     got = pl.pallas_call(
         functools.partial(kernel, n_ctx, n_dp, reduce_here),

time: 40 us -> 38.9 us (0.972)
  Pallas kernels: 39.2 us -> 38.1 us
    pallas_call x1, Pallas kernels: 37.1 us -> 36.1 us  [local(): pl.pallas_call(functools.partial(kernel, n_ctx, n_dp, reduce_here), out_s...]
where the time goes in v4:
time: 38.9 us; the launch traced here: 38.7 us
  Pallas kernels  38.1 us (98%)
  between operations  0.64 us (2%)
    pallas_call x1, Pallas kernels, local(): pl.pallas_call(functools.partial(kernel, n_ctx, n_dp, reduce_here), out_s...  36.1 us
    pallas_call x1, Pallas kernels, hand_over(): pl.pallas_call(functools.partial(hand_over_kernel, count), out_shape=[jax...  2.05 us

profile of v4, /device:TPU:0, one launch (start us, length us, event | category | flops | bytes accessed | tf_op | source)
XLA Modules:
  0.0 38.7 jit_solution(3409672486019497950)
XLA Ops:
  0.6 36.1 %shard_map.111 = (bf16[1,256,1024]{2,1,0:T(8,128)(2,1)}, bf16[1,256,128]{2,1,0:T(8,128)(2,1)}, bf16[1,256,128]{2,1,0:T(8,128)(2,1)}, bf16[8,128,128]{2,1,0:T(8,128)(2,1)}) custom-call(bf16[1,256,1024]{2,1,0:T(8,128)(2,1)} %refs_0_.1, bf16[1,256,128]{2,1,0:T(8,128)(2,1)} %refs_1_.1, bf16[1,256,128]{2,1,0:T(8,128)(2,1)} %refs_2_.1, ...), custom_call_target="tpu_custom_call" | custom-call | tf_op jit(solution)/shard_map/pallas_call | solution.py:357
  36.7 2.1 %shard_map.112 = (bf16[1,256,1024]{2,1,0:T(8,128)(2,1)}, bf16[1,256,128]{2,1,0:T(8,128)(2,1)}, bf16[1,256,128]{2,1,0:T(8,128)(2,1)}, f32[1024,128]{1,0:T(8,128)}) custom-call(bf16[1,256,1024]{2,1,0:T(8,128)(2,1)} %get-tuple-element.8.refs_0_, bf16[1,256,128]{2,1,0:T(8,128)(2,1)} %get-tuple-element.9.refs_1_, bf16[1,256,128]{2,1,0:T(8,128)(2,1)} %get-tuple-element.10.refs_2_, ...), custom_call_target="tpu_custom_call" | custom-call | tf_op jit(solution)/shard_map/pallas_call | solution.py:311

commit v5 on v4

--- a/solution.py
+++ b/solution.py
@@ -265,19 +265,27 @@
         over_x = [remote(gb.at[c], gb.at[c], ag_s.at[nz], ag_r.at[nz], at_x)]
         for copy in over_z + over_x:
             copy.start()
+        kept = []
+
+        def keep(slot, n):
+            kept.append(pltpu.make_async_copy(gb.at[slot], tot_out.at[slot], store.at[n]))
+            kept[-1].start()
+
+        keep(c, 3)
         for s in range(1, nz):
             over_z[s - 1].wait_recv()
             slot = lax.rem(z - s + nz, nz) * 2 + xx
             copy = remote(gb.at[slot], gb.at[slot], ag_s.at[nz + s], ag_r.at[nz + s], at_x)
             copy.start()
             over_x.append(copy)
-        for copy in over_x:
-            copy.wait_recv()
-        tot_store = pltpu.make_async_copy(gb, tot_out, store.at[3])
-        tot_store.start()
+            keep(slot, 3 + s)
+        for s in range(nz):
+            over_x[s].wait_recv()
+            keep(lax.rem(z - s + nz, nz) * 2 + 1 - xx, 3 + nz + s)
         for copy in [*first_out.values(), *second_out.values(), *out.values()] + over_z + over_x:
             copy.wait_send()
-        tot_store.wait()
+        for copy in kept:
+            copy.wait()
     else:
         dv_store = finish_dv()
         dq_store = finish_dq()
@@ -338,7 +346,7 @@
         full, small, small, full, full, pltpu.VMEM((QH, rows), F32), pltpu.VMEM((1, rows), jnp.int32),
         pltpu.VMEM((QH, rows), F32), small, small, pltpu.VMEM((QH, 2 * rows, rows), BF16), full,
         wide, wide, wide, wide, small, small, small, small, small, small,
-        dma((7,)), dma((4,)), dma((2,)), dma((2,)), dma((2,)), dma((2,)),
+        dma((7,)), dma((3 + n_ctx,)), dma((2,)), dma((2,)), dma((2,)), dma((2,)),
         pltpu.VMEM((QH, rows, rows), F32),
     ]
     if reduce_here:

time: 38.9 us -> 38.9 us (level)
  no operation moved by 1% of the time
where the time goes in v5:
time: 38.9 us; the launch traced here: 38.7 us
  Pallas kernels  38.1 us (98%)
  between operations  0.64 us (2%)
    pallas_call x1, Pallas kernels, local(): pl.pallas_call(functools.partial(kernel, n_ctx, n_dp, reduce_here), out_s...  36 us
    pallas_call x1, Pallas kernels, hand_over(): pl.pallas_call(functools.partial(hand_over_kernel, count), out_shape=[jax...  2.05 us

profile of v5, /device:TPU:0, one launch (start us, length us, event | category | flops | bytes accessed | tf_op | source)
XLA Modules:
  0.0 38.7 jit_solution(13924444981033292128)
XLA Ops:
  0.6 36.0 %shard_map.111 = (bf16[1,256,1024]{2,1,0:T(8,128)(2,1)}, bf16[1,256,128]{2,1,0:T(8,128)(2,1)}, bf16[1,256,128]{2,1,0:T(8,128)(2,1)}, bf16[8,128,128]{2,1,0:T(8,128)(2,1)}) custom-call(bf16[1,256,1024]{2,1,0:T(8,128)(2,1)} %refs_0_.1, bf16[1,256,128]{2,1,0:T(8,128)(2,1)} %refs_1_.1, bf16[1,256,128]{2,1,0:T(8,128)(2,1)} %refs_2_.1, ...), custom_call_target="tpu_custom_call" | custom-call | tf_op jit(solution)/shard_map/pallas_call | solution.py:365
  36.7 2.1 %shard_map.112 = (bf16[1,256,1024]{2,1,0:T(8,128)(2,1)}, bf16[1,256,128]{2,1,0:T(8,128)(2,1)}, bf16[1,256,128]{2,1,0:T(8,128)(2,1)}, f32[1024,128]{1,0:T(8,128)}) custom-call(bf16[1,256,1024]{2,1,0:T(8,128)(2,1)} %get-tuple-element.8.refs_0_, bf16[1,256,128]{2,1,0:T(8,128)(2,1)} %get-tuple-element.9.refs_1_, bf16[1,256,128]{2,1,0:T(8,128)(2,1)} %get-tuple-element.10.refs_2_, ...), custom_call_target="tpu_custom_call" | custom-call | tf_op jit(solution)/shard_map/pallas_call | solution.py:319
